TPU v7x, 32 devices: a whole 2x2x4 slice. The times are simulated.
32 devices in a mesh: groups: 2 (over y), adapt: 8 (over z, core), tensor: 2 (over x).
Axes of the slice: x: 2, y: 2, z: 4, core: 2. Of those that a mesh axis runs over, the one named last changes fastest.
Arguments:
- hidden: bfloat16 [512, 8192], P(('groups', 'adapt'), 'tensor'), parts along dimension 0, may hold values from -6 to 6
- queries: bfloat16 [512, 8192], P(('groups', 'adapt'), 'tensor'), parts along dimension 0, may hold values from -5 to 5
- key_value_cache: bfloat16 [512, 2, 512, 1024], P(('groups', 'adapt'), None, None, 'tensor'), parts along dimension 0, may hold values from -4 to 4
- key_value_weight: bfloat16 [8192, 2, 1024], P(None, None, 'tensor'), may hold values from -0.0625 to 0.0625
- adapter_down_weight: bfloat16 [8, 8192, 128], P('adapt', 'tensor'), may hold values from -0.0625 to 0.0625
- adapter_up_weight: bfloat16 [8, 2, 64, 1024], P('adapt', None, None, 'tensor'), may hold values from -0.75 to 0.75
- request_adapter_index: int32 [512, 1], P(('groups', 'adapt')), parts along dimension 0, may hold values from 0 to 7; in each aligned block of 32 rows (0 to 31, 32 to 63, ...) at most 4 rows name the same one
- lengths: int32 [512], P(('groups', 'adapt')), parts along dimension 0, may hold values from 2 to 512, as said below
Outputs:
- attention: bfloat16 [512, 8192], P(('groups', 'adapt'), 'tensor'), parts along dimension 0
- new_entries: bfloat16 [512, 2, 1024], P(('groups', 'adapt'), None, 'tensor'), parts along dimension 0
There are 2 independent parts, one for each index of `groups`. A program takes and returns all parts, laid end to end along the dimension named above; an argument that names none is the same for every part. Nothing has to cross between parts.
Inputs may be any that keep to these rules, and one draw needn't show every extreme that they name: `request_adapter_index`: every adapter is named by some request; among the 32 requests of one device no adapter is named more than 4 times, a bound that some block reaches. `lengths`: some request of every device has all 512 positions valid.
All inputs are finite; a program needn't handle non-finite values.
Results may differ from a plain program's by a relative error of at most 0.015.
Values may be sent and summed in bfloat16 or wider, within the bound.
A program may use at most 192 MiB of HBM per device.

v0:
```python
import jax
import jax.numpy as jnp
from jax import lax
from jax.sharding import PartitionSpec as P

HEAD_DIM = 128
GROUP = 8


ADAPTER_SCALE = 2.0
THETA = 500000.0


def rotary(fields, positions):
    half_dim = HEAD_DIM // 2
    freqs = THETA ** (-(jnp.arange(half_dim, dtype=jnp.float32) * 2.0) / HEAD_DIM)
    angles = positions.astype(jnp.float32)[:, None] * freqs[None, :]
    cosine = jnp.cos(angles)[:, None, :]
    sine = jnp.sin(angles)[:, None, :]
    first_half = fields[..., :half_dim]
    second_half = fields[..., half_dim:]
    return jnp.concatenate(
        [first_half * cosine - second_half * sine, second_half * cosine + first_half * sine], -1
    )


def one_head(query_block, cached_keys, cached_values, fresh_key, fresh_value, valid):
    scaling = 1.0 / jnp.sqrt(jnp.float32(HEAD_DIM))
    scores = (
        jnp.einsum("rih,rph->rip", query_block, cached_keys, preferred_element_type=jnp.float32)
        * scaling
    )
    own_score = (
        jnp.einsum("rih,rh->ri", query_block, fresh_key, preferred_element_type=jnp.float32)
        * scaling
    )
    scores = jnp.where(valid, scores, jnp.float32(-1e30))
    highest = jnp.maximum(jnp.max(scores, -1), own_score)
    weights = jnp.where(valid, jnp.exp(scores - highest[..., None]), jnp.float32(0.0))
    own_weight = jnp.exp(own_score - highest)
    totals = jnp.sum(weights, -1) + own_weight
    probs = (weights / totals[..., None]).astype(jnp.bfloat16)
    own_prob = (own_weight / totals).astype(jnp.bfloat16)
    mixed = jnp.einsum("rip,rph->rih", probs, cached_values, preferred_element_type=jnp.float32)
    mixed = (
        mixed
        + own_prob.astype(jnp.float32)[..., None] * fresh_value.astype(jnp.float32)[:, None, :]
    )
    return mixed.reshape(mixed.shape[0], GROUP * HEAD_DIM).astype(jnp.bfloat16)


def on_device(
    hidden,
    queries,
    key_value_cache,
    key_value_weight,
    adapter_down_weight,
    adapter_up_weight,
    request_adapter_index,
    lengths,
):
    requests_here = hidden.shape[0]
    head_cols = key_value_weight.shape[2]
    heads_here = head_cols // HEAD_DIM
    gathered = lax.all_gather(hidden, "tensor", axis=1, tiled=True)
    base = jnp.dot(
        gathered,
        key_value_weight.reshape(key_value_weight.shape[0], 2 * head_cols),
        preferred_element_type=jnp.float32,
    ).reshape(requests_here, 2, head_cols)
    picked_adapter_index = request_adapter_index[:, 0]
    rank_columns = adapter_down_weight.shape[2]
    rank_half = rank_columns // 2
    update_parts = lax.all_gather(adapter_down_weight, "adapt", axis=0, tiled=True)
    products = jnp.einsum("zf,qfv->zqv", hidden, update_parts, preferred_element_type=jnp.float32)
    selector = (
        picked_adapter_index[:, None] == jnp.arange(update_parts.shape[0], dtype=jnp.int32)[None, :]
    ).astype(jnp.float32)
    partial_rows = jnp.einsum("rac,ra->rc", products, selector)
    shrunk = lax.psum(partial_rows, "tensor").astype(jnp.bfloat16)
    low_rows = shrunk.reshape(requests_here, 2, rank_half)
    update_parts = lax.all_gather(adapter_up_weight, "adapt", axis=0, tiled=True)
    products = jnp.einsum(
        "rtc,atcx->ratx", low_rows, update_parts, preferred_element_type=jnp.float32
    )
    selector = (
        picked_adapter_index[:, None] == jnp.arange(update_parts.shape[0], dtype=jnp.int32)[None, :]
    ).astype(jnp.float32)
    raised_update = jnp.einsum("ratx,ra->rtx", products, selector)
    adapter_update = (ADAPTER_SCALE * raised_update).astype(jnp.bfloat16)
    fresh = base + adapter_update.astype(jnp.float32)
    keys = rotary(fresh[:, 0].reshape(requests_here, heads_here, HEAD_DIM), lengths).reshape(
        requests_here, head_cols
    )
    new_entries = jnp.stack([keys, fresh[:, 1]], 1).astype(jnp.bfloat16)
    context = key_value_cache.shape[2]
    valid = (jnp.arange(context, dtype=jnp.int32)[None, :] < lengths[:, None])[:, None, :]
    query_cols = GROUP * HEAD_DIM
    outputs = []
    for head in range(heads_here):
        low = head * HEAD_DIM
        query_block = queries[:, head * query_cols : (head + 1) * query_cols].reshape(
            requests_here, GROUP, HEAD_DIM
        )
        cached_keys = key_value_cache[:, 0, :, low : low + HEAD_DIM]
        cached_values = key_value_cache[:, 1, :, low : low + HEAD_DIM]
        fresh_key = new_entries[:, 0, low : low + HEAD_DIM]
        fresh_value = new_entries[:, 1, low : low + HEAD_DIM]
        outputs.append(
            one_head(query_block, cached_keys, cached_values, fresh_key, fresh_value, valid)
        )
    attention = outputs[0] if heads_here == 1 else jnp.concatenate(outputs, -1)
    return (attention, new_entries)


def solution(mesh):
    in_specs = (
        P(("groups", "adapt"), "tensor"),
        P(("groups", "adapt"), "tensor"),
        P(("groups", "adapt"), None, None, "tensor"),
        P(None, None, "tensor"),
        P("adapt", "tensor", None),
        P("adapt", None, None, "tensor"),
        P(("groups", "adapt"), None),
        P(("groups", "adapt")),
    )
    out_specs = (P(("groups", "adapt"), "tensor"), P(("groups", "adapt"), None, "tensor"))
    return jax.shard_map(
        on_device, mesh=mesh, in_specs=in_specs, out_specs=out_specs, check_vma=False
    )
```

profile of v0, /device:TPU:0, one launch (start us, length us, event | category | flops | bytes accessed | tf_op | source)
XLA Modules:
  0.0 151.4 jit_solution(433679833950454424)
XLA Ops:
  7.2 0.0 all-gather.3.cloned.1.call-start
  7.2 0.7 all-gather.3.cloned.1.call-update
  7.9 0.0 all-gather.5.cloned.1.call-start
  7.9 0.7 all-gather.5.cloned.1.call-update
  8.7 0.7 convert_element_type.86
  9.3 0.7 iota_compare_fusion
  10.1 0.7 fusion.104
  10.8 1.0 slice_bitcast_fusion.1
  11.8 0.1 multiply_cosine_fusion
  11.9 3.5 %fusion.133 = (f32[32,8]{1,0:T(8,128)S(1)}, f32[32,8,512]{2,1,0:T(8,128)S(1)}) fusion(bf16[32,8,128]{2,1,0:T(8,128)(2,1)S(1)} %bitcast.192, bf16[32,2,512,512]{3,2,1,0:T(8,128)(2,1)} %param.10, pred[32,512]{1,0:T(8,128)(4,1)S(1)} %iota_compare_fusion), kind=kOutput, calls=%fused_computation.150 | convolution fusion | flops 33947392 | bytes 4801536 | tf_op jit(solution)/shard_map/rih,rph->rip/dot_general | solution.py:30
  15.4 10.2 %all_gather.9 = bf16[32,8192]{1,0:T(8,128)(2,1)S(1)} all-gather(bf16[32,4096]{1,0:T(8,128)(2,1)} %param.8), channel_id=1, replica_groups=mesh['groups'=2,'adapt'=8,'tensor'=2] {'tensor'}, dimensions={1}, use_global_device_ids=true | all-gather | bytes 786432 | tf_op jit(solution)/shard_map/all_gather | solution.py:65
  25.6 16.6 %copy.57 = bf16[1024,8,2,512]{3,1,2,0:T(8,128)(2,1)} copy(bf16[1024,8,2,512]{3,2,1,0:T(2,128)(2,1)} %bitcast.191) | data formatting | bytes 33554432
  42.2 0.0 copy-start
  42.2 21.1 %copy.21 = bf16[1024,8192]{1,0:T(8,128)(2,1)} copy(bf16[1024,8192]{0,1:T(8,128)(2,1)} %bitcast.190) | data formatting | bytes 33554432 | tf_op jit(solution)/shard_map/dot_general | solution.py:66
  63.3 3.5 %fusion.131 = (f32[32,8]{1,0:T(8,128)S(1)}, f32[32,8,512]{2,1,0:T(8,128)S(1)}) fusion(bf16[32,8,128]{2,1,0:T(8,128)(2,1)S(1)} %bitcast.198, bf16[32,2,512,512]{3,2,1,0:T(8,128)(2,1)} %param.10, pred[32,512]{1,0:T(8,128)(4,1)S(1)} %iota_compare_fusion), kind=kOutput, calls=%fused_computation.148 | convolution fusion | flops 33947392 | bytes 4801536 | tf_op jit(solution)/shard_map/rih,rph->rip/dot_general | solution.py:30
  66.8 3.5 %fusion.132 = (f32[32,8]{1,0:T(8,128)S(1)}, f32[32,8,512]{2,1,0:T(8,128)S(1)}) fusion(bf16[32,8,128]{2,1,0:T(8,128)(2,1)S(1)} %bitcast.196, bf16[32,2,512,512]{3,2,1,0:T(8,128)(2,1)} %param.10, pred[32,512]{1,0:T(8,128)(4,1)S(1)} %iota_compare_fusion), kind=kOutput, calls=%fused_computation.149 | convolution fusion | flops 33947392 | bytes 4801536 | tf_op jit(solution)/shard_map/rih,rph->rip/dot_general | solution.py:30
  70.4 3.6 %fusion.130 = (f32[32,8]{1,0:T(8,128)S(1)}, f32[32,8,512]{2,1,0:T(8,128)S(1)}) fusion(bf16[32,8,128]{2,1,0:T(8,128)(2,1)S(1)} %bitcast.194, bf16[32,2,512,512]{3,2,1,0:T(8,128)(2,1)} %param.10, pred[32,512]{1,0:T(8,128)(4,1)S(1)} %iota_compare_fusion), kind=kOutput, calls=%fused_computation.147 | convolution fusion | flops 33947392 | bytes 4801536 | tf_op jit(solution)/shard_map/rih,rph->rip/dot_general | solution.py:30
  73.9 20.5 %all-gather.3.cloned.1.call-done = bf16[8,4096,128]{2,1,0:T(8,128)(2,1)} async-done(((bf16[1,4096,128]{2,1,0:T(8,128)(2,1)}), bf16[8,4096,128]{2,1,0:T(8,128)(2,1)}) %all-gather.3.cloned.1.call-update) | async-done | bytes 8388624 | tf_op jit(solution)/shard_map/all_gather | solution.py:74
  94.4 0.0 copy-done
  94.4 4.8 %fusion.80 = bf16[32,8,128]{2,0,1:T(8,128)(2,1)S(1)} fusion(bf16[8,4096,128]{2,1,0:T(8,128)(2,1)} %all-gather.3.cloned.1.call-done, bf16[32,4096]{1,0:T(8,128)(2,1)S(1)} %copy-done), kind=kOutput, calls=%fused_computation.59 | convolution fusion | flops 268435456 | bytes 8716288 | tf_op jit(solution)/shard_map/zf,qfv->zqv/dot_general | solution.py:75
  99.2 0.2 fusion.99
  99.4 8.2 %psum.7 = bf16[32,128]{1,0:T(8,128)(2,1)S(1)} all-reduce(f32[32,128]{1,0:T(8,128)S(1)} %bitcast.216), channel_id=1, replica_groups=mesh['groups'=2,'adapt'=8,'tensor'=2] {'tensor'}, use_global_device_ids=true, to_apply=%region_1.2 | all-reduce | flops 4096 | bytes 24576 | tf_op jit(solution)/shard_map/psum | solution.py:80
  107.6 0.1 reshape.127
  107.7 9.0 %all-gather.5.cloned.1.call-done = bf16[8,2,64,512]{3,2,1,0:T(8,128)(2,1)} async-done(((bf16[1,2,64,512]{3,2,1,0:T(8,128)(2,1)}), bf16[8,2,64,512]{3,2,1,0:T(8,128)(2,1)}) %all-gather.5.cloned.1.call-update) | async-done | bytes 1048592 | tf_op jit(solution)/shard_map/all_gather | solution.py:82
  116.7 1.5 convolution_bitcast_fusion
  118.2 0.4 fusion.72
  118.6 10.8 %fusion.134 = (bf16[32,2,512]{2,0,1:T(8,128)(2,1)S(1)}, f32[32,2,512]{2,0,1:T(8,128)S(1)}) fusion(f32[32,1,2,512]{3,1,2,0:T(1,128)S(1)} %fusion.72, bf16[2,512,8192]{2,1,0:T(8,128)(2,1)} %bitcast.189, bf16[32,8192]{1,0:T(8,128)(2,1)S(1)} %all_gather.9), kind=kOutput, calls=%fused_computation.151 | convolution fusion | flops 537034752 | bytes 17629184 | tf_op jit(solution)/shard_map/dot_general | solution.py:66
  129.5 0.1 subtract_convert_fusion
  129.6 0.1 pad_maximum_fusion.2
  129.8 0.1 fusion.106
  129.9 0.2 fusion.110
  130.1 0.2 fusion.108
  130.2 0.2 fusion.112
  130.5 0.7 fusion.76
  131.2 2.9 %fusion.69 = bf16[32,8,128]{2,1,0:T(8,128)(2,1)S(1)} fusion(bf16[32,2,512,512]{3,2,1,0:T(8,128)(2,1)} %param.10, f32[32,8,512]{2,1,0:T(8,128)S(1)} %get-tuple-element.37, f32[32,8]{1,0:T(8,128)S(1)} %get-tuple-element.21, f32[32,8]{1,0:T(8,128)S(1)} %multiply_maximum_fusion.3, pred[32,512]{1,0:T(8,128)(4,1)S(1)} %iota_compare_fusion, ...), kind=kOutput, calls=%fused_computation.41 | convolution fusion | flops 34177024 | bytes 4819968 | tf_op jit(solution)/shard_map/rip,rph->rih/dot_general | solution.py:44
  134.2 2.9 %fusion.66 = bf16[32,8,128]{2,1,0:T(8,128)(2,1)S(1)} fusion(bf16[32,2,512,512]{3,2,1,0:T(8,128)(2,1)} %param.10, f32[32,8,512]{2,1,0:T(8,128)S(1)} %get-tuple-element.39, f32[32,8]{1,0:T(8,128)S(1)} %get-tuple-element.46, f32[32,8]{1,0:T(8,128)S(1)} %multiply_maximum_fusion.2, pred[32,512]{1,0:T(8,128)(4,1)S(1)} %iota_compare_fusion, ...), kind=kOutput, calls=%fused_computation.40 | convolution fusion | flops 34177024 | bytes 4819968 | tf_op jit(solution)/shard_map/rip,rph->rih/dot_general | solution.py:44
  137.2 2.9 %fusion.63 = bf16[32,8,128]{2,1,0:T(8,128)(2,1)S(1)} fusion(bf16[32,2,512,512]{3,2,1,0:T(8,128)(2,1)} %param.10, f32[32,8,512]{2,1,0:T(8,128)S(1)} %get-tuple-element.41, f32[32,8]{1,0:T(8,128)S(1)} %get-tuple-element.25, f32[32,8]{1,0:T(8,128)S(1)} %multiply_maximum_fusion.1, pred[32,512]{1,0:T(8,128)(4,1)S(1)} %iota_compare_fusion, ...), kind=kOutput, calls=%fused_computation.39 | convolution fusion | flops 34177024 | bytes 4819968 | tf_op jit(solution)/shard_map/rip,rph->rih/dot_general | solution.py:44
  140.1 2.9 %fusion.60 = bf16[32,8,128]{2,1,0:T(8,128)(2,1)S(1)} fusion(bf16[32,2,512,512]{3,2,1,0:T(8,128)(2,1)} %param.10, f32[32,8,512]{2,1,0:T(8,128)S(1)} %get-tuple-element.43, f32[32,8]{1,0:T(8,128)S(1)} %get-tuple-element.48, f32[32,8]{1,0:T(8,128)S(1)} %multiply_maximum_fusion, pred[32,512]{1,0:T(8,128)(4,1)S(1)} %iota_compare_fusion, ...), kind=kOutput, calls=%fused_computation.38 | convolution fusion | flops 34177024 | bytes 4819968 | tf_op jit(solution)/shard_map/rip,rph->rih/dot_general | solution.py:44
  143.1 0.7 copy.29
  143.8 0.7 pad_maximum_fusion
  (22 shorter events, 0.3 us)
Async XLA Ops:
  7.2 87.2 %all-gather.3.cloned.1.call-start = ((), (), s32[]{:S(2)}) async-start(), calls=%async_computation | async-start | bytes 9437184 | tf_op jit(solution)/shard_map/all_gather | solution.py:74
  7.9 108.8 %all-gather.5.cloned.1.call-start = ((), (), s32[]{:S(2)}) async-start(), calls=%async_computation.1 | async-start | bytes 1179648 | tf_op jit(solution)/shard_map/all_gather | solution.py:82
  42.2 52.2 %copy-start = (bf16[32,4096]{1,0:T(8,128)(2,1)S(1)}, bf16[32,4096]{1,0:T(8,128)(2,1)}, u32[]{:S(2)}) copy-start(bf16[32,4096]{1,0:T(8,128)(2,1)} %param.8) | copy-start | bytes 786436
Sparse Core Ops, SparseCore 0:
  9.6 84.7 all-gather.2
  96.0 20.6 all-gather.4
where the time goes:
time: 153 us; the launch traced here: 151 us
  matrix products  44.3 us (29%)
  local copies, waits for them, and re-layouts  39.6 us (26%)
  waiting for transfers between devices  30.8 us (20%)
  blocking collectives  18.4 us (12%)
  between operations  14.3 us (9%)
  other arithmetic  3.99 us (3%)
    dot_general x1, local copies, waits for them, and re-layouts, on_device(): jnp.dot(gathered, key_value_weight.reshape(key_value_weight.shape[0], 2 *...  21.1 us
    all_gather x1, waiting for transfers between devices, on_device(): lax.all_gather(adapter_down_weight, 'adapt', axis=0, tiled=True)  20.5 us
    unnamed x13, local copies, waits for them, and re-layouts  18.4 us
    dot_general x4, matrix products, one_head(): jnp.einsum('rih,rph->rip', query_block, cached_keys, preferred_element_ty...  14.1 us
    dot_general x4, matrix products, one_head(): jnp.einsum('rip,rph->rih', probs, cached_values, preferred_element_type=j...  11.8 us
    dot_general x1, matrix products, on_device(): jnp.dot(gathered, key_value_weight.reshape(key_value_weight.shape[0], 2 *...  10.8 us
    all_gather x1, blocking collectives, on_device(): gathered = lax.all_gather(hidden, 'tensor', axis=1, tiled=True)  10.2 us
    all_gather x1, waiting for transfers between devices, on_device(): lax.all_gather(adapter_up_weight, 'adapt', axis=0, tiled=True)  8.98 us
  transfers between devices with their start and end apart: 2, of which 2 were waited for; matrix products, arithmetic and copies ran while one was open for 40% of the time, Pallas kernels for 0%

commit v1 on v0

v1 whole, which is shorter than its diff:
```python
import functools

import jax
import jax.numpy as jnp
from jax import lax
from jax.experimental import pallas as pl
from jax.experimental.pallas import tpu as pltpu
from jax.sharding import PartitionSpec as P

HEAD_DIM = 128
GROUP = 8
MOST = 4
ADAPTER_SCALE = 2.0
THETA = 500000.0
ROWS = 16
CUT = ROWS // MOST
DEPTH = 512
SLOTS = 4
CHUNK = 128
AHEAD = 8
MESH = pl.DeviceIdType.MESH
F32 = jnp.float32
BF16 = jnp.bfloat16


def one_hot(condition):
    return jnp.where(condition, 1.0, 0.0).astype(BF16)


def iota(shape, dim):
    return lax.broadcasted_iota(jnp.int32, shape, dim)


def entries_kernel(
    adapters, tensors,
    hidden, weight, down, up, index_col, index_row, cosine, sine, out,
    blocks, wide, gathered, sent, taken, partial, back_sent, back, down_here, up_here, total,
    block_sem, local_sem, hs, hr, ds, dr, ps, pr, rs, rr,
):
    me = lax.axis_index("adapt")
    side = lax.axis_index("tensor")
    rows, local = hidden.shape
    cols = out.shape[2]
    tiles = cols // 128
    per_source = local // DEPTH
    count = per_source * tensors
    piece = local // CUT

    def block_copies(n):
        source = lax.rem(side + tensors - n // per_source, tensors)
        start = pl.multiple_of(source * local + lax.rem(n, per_source) * DEPTH, DEPTH)
        slot = lax.rem(n, SLOTS)
        return [
            pltpu.make_async_copy(
                weight.at[pl.ds(start, DEPTH), :, pl.ds(tile * 128, 128)],
                blocks.at[slot, tile],
                block_sem.at[slot, tile],
            )
            for tile in range(tiles)
        ]

    down_copy = pltpu.make_async_copy(down.at[0], down_here, local_sem.at[0])
    up_copy = pltpu.make_async_copy(up.at[0], up_here, local_sem.at[1])

    barrier = pltpu.get_barrier_semaphore()
    for j in range(1, adapters):
        pl.semaphore_signal(
            barrier, inc=1, device_id={"adapt": lax.rem(me + j, adapters)}, device_id_type=MESH
        )
    for j in range(1, tensors):
        pl.semaphore_signal(
            barrier, inc=1, device_id={"tensor": lax.rem(side + j, tensors)}, device_id_type=MESH
        )
    for n in range(SLOTS):
        for copy in block_copies(jnp.int32(n)):
            copy.start()
    down_copy.start()
    up_copy.start()

    col = index_col[...]
    row = index_row[...]
    same = col == row
    first, second = iota((rows, rows), 0), iota((rows, rows), 1)
    place_col = jnp.sum(jnp.where(same & (second < first), 1.0, 0.0), axis=1, keepdims=True)
    place_row = jnp.sum(jnp.where(same & (first < second), 1.0, 0.0), axis=0, keepdims=True)
    place_col = place_col.astype(jnp.int32)
    place_row = place_row.astype(jnp.int32)

    high = adapters * ROWS
    line = iota((high, rows), 0)
    wanted = (line // ROWS == row) & (line % MOST == place_row)
    packed = jnp.zeros((high, piece), F32)
    for q in range(CUT):
        pick = one_hot(wanted & (line % ROWS // MOST == q))
        packed += jnp.dot(
            pick, hidden[:, q * piece : (q + 1) * piece], preferred_element_type=F32
        )
    sent[...] = packed.astype(BF16)
    here = pl.ds(pl.multiple_of(me * ROWS, ROWS), ROWS)

    pl.semaphore_wait(barrier, adapters - 1 + tensors - 1)

    def block_of(j):
        return pl.ds(pl.multiple_of(lax.rem(me + j, adapters) * ROWS, ROWS), ROWS)

    out_copies, back_copies = [None], [None]
    for j in range(1, adapters):
        copy = pltpu.make_async_remote_copy(
            src_ref=sent.at[block_of(j)],
            dst_ref=taken.at[here],
            send_sem=ds.at[j],
            recv_sem=dr.at[j],
            device_id={"adapt": lax.rem(me + j, adapters)},
            device_id_type=MESH,
        )
        copy.start()
        out_copies.append(copy)
    hidden_copies, sum_copies = [None], [None]
    for j in range(1, tensors):
        copy = pltpu.make_async_remote_copy(
            src_ref=hidden,
            dst_ref=gathered.at[j],
            send_sem=hs.at[j],
            recv_sem=hr.at[j],
            device_id={"tensor": lax.rem(side + j, tensors)},
            device_id_type=MESH,
        )
        copy.start()
        hidden_copies.append(copy)
    taken[here] = sent[here]
    total[...] = jnp.zeros_like(total)

    spread = iota((128, 256), 1) - 2 * iota((128, 256), 0)
    even, odd = one_hot(spread == 0), one_hot(spread == 1)

    def widen(source):
        for at in range(local // 128):
            part = source[:, at * 128 : (at + 1) * 128]
            to = slice(at * 256, (at + 1) * 256)
            wide[:rows, to] = jnp.dot(part, even, preferred_element_type=F32).astype(BF16)
            wide[rows:, to] = jnp.dot(part, odd, preferred_element_type=F32).astype(BF16)

    def stream(low, top):
        def step(n, carry):
            slot = lax.rem(n, SLOTS)
            start = pl.multiple_of(lax.rem(n, per_source) * 2 * DEPTH, 2 * DEPTH)
            features = wide[:, pl.ds(start, 2 * DEPTH)]
            for tile, copy in enumerate(block_copies(n)):
                copy.wait()
                total[:, tile * 128 : (tile + 1) * 128] += jnp.dot(
                    features,
                    blocks.at[slot, tile].reshape(2 * DEPTH, 128)[...],
                    preferred_element_type=F32,
                )

            @pl.when(n + SLOTS < count)
            def _():
                for copy in block_copies(n + SLOTS):
                    copy.start()

            return carry

        lax.fori_loop(low, top, step, 0)

    widen(hidden)
    stream(0, per_source)

    for j in range(1, adapters):
        out_copies[j].wait_recv()
    down_copy.wait()
    arrived = taken[...]
    which = iota((high, 128), 0) % ROWS // MOST
    grown = jnp.zeros((high, 128), F32)
    for q in range(CUT):
        product = jnp.dot(
            arrived, down_here[q * piece : (q + 1) * piece, :], preferred_element_type=F32
        )
        grown = jnp.where(which == q, product, grown)
    short = adapters * MOST
    to, fro = iota((short, high), 0), iota((short, high), 1)
    fold = (to // MOST == fro // ROWS) & (to % MOST == fro % MOST)
    partial[0] = jnp.dot(
        jnp.where(fold, 1.0, 0.0), grown,
        preferred_element_type=F32, precision=lax.Precision.HIGHEST,
    )
    for j in range(1, tensors):
        copy = pltpu.make_async_remote_copy(
            src_ref=partial.at[0],
            dst_ref=partial.at[j],
            send_sem=ps.at[j],
            recv_sem=pr.at[j],
            device_id={"tensor": lax.rem(side + j, tensors)},
            device_id_type=MESH,
        )
        copy.start()
        sum_copies.append(copy)

    hidden_copies[1].wait_recv()
    widen(gathered.at[1])
    middle = per_source + per_source // 2
    stream(per_source, middle)

    up_copy.wait()
    rank_sum = partial[0]
    for j in range(1, tensors):
        sum_copies[j].wait_recv()
        rank_sum = rank_sum + partial[j]
    shrunk = rank_sum.astype(BF16)
    half = up_here.shape[1]
    to, fro = iota((high, short), 0), iota((high, short), 1)
    returned = jnp.zeros((high, cols), F32)
    for t in range(2):
        raised = jnp.dot(
            shrunk[:, t * half : (t + 1) * half], up_here[t], preferred_element_type=F32
        )
        raised = (ADAPTER_SCALE * raised).astype(BF16)
        put = (to // ROWS == fro // MOST) & (to % ROWS == fro % MOST + t * MOST)
        returned += jnp.dot(one_hot(put), raised, preferred_element_type=F32)
    back_sent[...] = returned.astype(BF16)
    for j in range(1, adapters):
        copy = pltpu.make_async_remote_copy(
            src_ref=back_sent.at[block_of(j)],
            dst_ref=back.at[here],
            send_sem=rs.at[j],
            recv_sem=rr.at[j],
            device_id={"adapt": lax.rem(me + j, adapters)},
            device_id_type=MESH,
        )
        copy.start()
        back_copies.append(copy)
    back[here] = back_sent[here]

    stream(middle, 2 * per_source)
    for j in range(2, tensors):
        hidden_copies[j].wait_recv()
        widen(gathered.at[j])
        stream(j * per_source, (j + 1) * per_source)

    for j in range(1, adapters):
        back_copies[j].wait_recv()
    updates = back[...]
    line = iota((rows, high), 1)
    for t in range(2):
        choose = one_hot((line // ROWS == col) & (line % ROWS == place_col + t * MOST))
        fresh = total[t * rows : (t + 1) * rows, :] + jnp.dot(
            choose, updates, preferred_element_type=F32
        )
        for head in range(cols // HEAD_DIM):
            at = slice(head * HEAD_DIM, (head + 1) * HEAD_DIM)
            part = fresh[:, at]
            if t == 0:
                part = part * cosine[...] + pltpu.roll(part, HEAD_DIM // 2, 1) * sine[...]
            out[t, :, at] = part.astype(BF16).astype(F32)

    for j in range(1, adapters):
        out_copies[j].wait_send()
        back_copies[j].wait_send()
    for j in range(1, tensors):
        hidden_copies[j].wait_send()
        sum_copies[j].wait_send()


def entries_of(adapters, tensors, hidden, weight, down, up, index, cosine, sine):
    rows, local = hidden.shape
    cols = weight.shape[2]
    high = adapters * ROWS
    dma = pltpu.SemaphoreType.DMA
    vmem = pl.BlockSpec(memory_space=pltpu.VMEM)
    hbm = pl.BlockSpec(memory_space=pl.ANY)
    return pl.pallas_call(
        functools.partial(entries_kernel, adapters, tensors),
        out_shape=jax.ShapeDtypeStruct((2, rows, cols), F32),
        in_specs=[vmem, hbm, hbm, hbm, vmem, vmem, vmem, vmem],
        out_specs=vmem,
        scratch_shapes=[
            pltpu.VMEM((SLOTS, cols // 128, DEPTH, 2, 128), BF16),
            pltpu.VMEM((2 * rows, 2 * local), BF16),
            pltpu.VMEM((tensors, rows, local), BF16),
            pltpu.VMEM((high, local // CUT), BF16),
            pltpu.VMEM((high, local // CUT), BF16),
            pltpu.VMEM((tensors, adapters * MOST, 128), F32),
            pltpu.VMEM((high, cols), BF16),
            pltpu.VMEM((high, cols), BF16),
            pltpu.VMEM(down.shape[1:], BF16),
            pltpu.VMEM(up.shape[1:], BF16),
            pltpu.VMEM((2 * rows, cols), F32),
            dma((SLOTS, cols // 128)),
            dma((2,)),
            dma((tensors,)), dma((tensors,)),
            dma((adapters,)), dma((adapters,)),
            dma((tensors,)), dma((tensors,)),
            dma((adapters,)), dma((adapters,)),
        ],
        compiler_params=pltpu.CompilerParams(
            collective_id=0, has_side_effects=True, vmem_limit_bytes=40 << 20
        ),
        name="entries",
    )(hidden, weight, down, up, index, index.reshape(1, rows), cosine, sine)


def attend_kernel(lengths, queries, cache, entries, out, held, sems):
    requests, lines, _ = queries.shape
    context = cache.shape[2]
    heads = lines // GROUP
    chunks = context // CHUNK
    scaling = HEAD_DIM ** -0.5

    def copies(r, act):
        slot = lax.rem(r, AHEAD)
        for c in range(chunks):
            @pl.when(c * CHUNK < lengths[r])
            def _():
                act(
                    pltpu.make_async_copy(
                        cache.at[r, :, pl.ds(c * CHUNK, CHUNK), :],
                        held.at[slot, :, pl.ds(c * CHUNK, CHUNK), :],
                        sems.at[slot, c],
                    )
                )

    for r in range(AHEAD):
        copies(r, lambda copy: copy.start())

    owner = iota((lines, HEAD_DIM), 0) // GROUP

    def own(fields):
        chosen = jnp.zeros((lines, HEAD_DIM), F32)
        for head in range(heads):
            part = fields[:, head * HEAD_DIM : (head + 1) * HEAD_DIM]
            chosen = jnp.where(owner == head, part, chosen)
        return chosen

    def step(r, carry):
        slot = lax.rem(r, AHEAD)
        copies(r, lambda copy: copy.wait())
        length = lengths[r]
        query = queries[r]
        apart = jnp.concatenate(
            [jnp.where(owner == head, query, 0).astype(BF16) for head in range(heads)], 1
        )
        own_score = jnp.sum(
            query.astype(F32) * own(entries[0, pl.ds(r, 1), :]), axis=1, keepdims=True
        ) * scaling
        own_value = own(entries[1, pl.ds(r, 1), :])

        for used in range(1, chunks + 1):
            @pl.when((length > (used - 1) * CHUNK) & (length <= used * CHUNK))
            def _():
                size = used * CHUNK
                scores = lax.dot_general(
                    apart, held[slot, 0, :size, :], (((1,), (1,)), ((), ())),
                    preferred_element_type=F32,
                ) * scaling
                valid = iota((lines, size), 1) < length
                scores = jnp.where(valid, scores, -1e30)
                highest = jnp.maximum(jnp.max(scores, axis=1, keepdims=True), own_score)
                weights = jnp.where(valid, jnp.exp(scores - highest), 0.0)
                own_weight = jnp.exp(own_score - highest)
                inverse = 1.0 / (jnp.sum(weights, axis=1, keepdims=True) + own_weight)
                probs = (weights * inverse).astype(BF16)
                own_prob = (own_weight * inverse).astype(BF16).astype(F32)
                mixed = own(
                    jnp.dot(probs, held[slot, 1, :size, :], preferred_element_type=F32)
                )
                out[r] = (mixed + own_prob * own_value).astype(BF16)

        @pl.when(r + AHEAD < requests)
        def _():
            copies(r + AHEAD, lambda copy: copy.start())

        return carry

    lax.fori_loop(0, requests, step, 0)


def attend(lengths, queries, cache, entries):
    requests, _, context, cols = cache.shape
    vmem = pl.BlockSpec(memory_space=pltpu.VMEM)
    return pl.pallas_call(
        attend_kernel,
        out_shape=jax.ShapeDtypeStruct(queries.shape, BF16),
        in_specs=[
            pl.BlockSpec(memory_space=pltpu.SMEM), vmem, pl.BlockSpec(memory_space=pl.ANY), vmem
        ],
        out_specs=vmem,
        scratch_shapes=[
            pltpu.VMEM((AHEAD, 2, context, cols), BF16),
            pltpu.SemaphoreType.DMA((AHEAD, context // CHUNK)),
        ],
        compiler_params=pltpu.CompilerParams(vmem_limit_bytes=40 << 20),
        name="attend",
    )(lengths, queries, cache, entries)


def on_device(
    adapters, tensors,
    hidden, queries, key_value_cache, key_value_weight,
    adapter_down_weight, adapter_up_weight, request_adapter_index, lengths,
):
    requests = hidden.shape[0]
    half = HEAD_DIM // 2
    freqs = THETA ** (-(jnp.arange(half, dtype=F32) * 2.0) / HEAD_DIM)
    angles = lengths.astype(F32)[:, None] * freqs[None, :]
    cosine = jnp.concatenate([jnp.cos(angles)] * 2, -1)
    sine = jnp.sin(angles)
    sine = jnp.concatenate([-sine, sine], -1)
    entries = entries_of(
        adapters, tensors, hidden, key_value_weight, adapter_down_weight, adapter_up_weight,
        request_adapter_index, cosine, sine,
    )
    attention = attend(
        lengths, queries.reshape(requests, -1, HEAD_DIM), key_value_cache, entries
    )
    return (
        attention.reshape(requests, -1),
        jnp.swapaxes(entries, 0, 1).astype(BF16),
    )


def solution(mesh):
    in_specs = (
        P(("groups", "adapt"), "tensor"),
        P(("groups", "adapt"), "tensor"),
        P(("groups", "adapt"), None, None, "tensor"),
        P(None, None, "tensor"),
        P("adapt", "tensor", None),
        P("adapt", None, None, "tensor"),
        P(("groups", "adapt"), None),
        P(("groups", "adapt")),
    )
    out_specs = (P(("groups", "adapt"), "tensor"), P(("groups", "adapt"), None, "tensor"))
    return jax.shard_map(
        functools.partial(on_device, mesh.shape["adapt"], mesh.shape["tensor"]),
        mesh=mesh, in_specs=in_specs, out_specs=out_specs, check_vma=False,
    )
```

time: 153 us -> 55.9 us (0.37)
  Pallas kernels: 0 us -> 46.4 us
  matrix products: 44.3 us -> 0 us
  local copies, waits for them, and re-layouts: 39.6 us -> 7.62 us
  waiting for transfers between devices: 30.8 us -> 0 us
  blocking collectives: 18.4 us -> 0 us
  between operations: 14.3 us -> 0.68 us
  other arithmetic: 3.99 us -> 0.9 us
    pallas_call x0 -> x2, Pallas kernels: none -> 46.4 us  [the longest x1 25.6 us: entries_of(): pl.pallas_call(functools.partial(entries_kernel, adapters, tensors), out_...]
    dot_general x17 -> x0, matrix products: 44.3 us -> none  [the longest x4 14.1 us: one_head(): jnp.einsum('rih,rph->rip', query_block, cached_keys, preferred_element_ty...]
    all_gather x2 -> x0, waiting for transfers between devices: 29.4 us -> none  [the longest x1 20.5 us: on_device(): lax.all_gather(adapter_down_weight, 'adapt', axis=0, tiled=True)]
    dot_general x1 -> x0, local copies, waits for them, and re-layouts: 21.1 us -> none  [on_device(): jnp.dot(gathered, key_value_weight.reshape(key_value_weight.shape[0], 2 *...]
    unnamed x13 -> x14, local copies, waits for them, and re-layouts: 18.4 us -> 7.62 us
    all_gather x1 -> x0, blocking collectives: 10.2 us -> none  [on_device(): gathered = lax.all_gather(hidden, 'tensor', axis=1, tiled=True)]
    psum x1 -> x0, blocking collectives: 8.18 us -> none  [on_device(): shrunk = lax.psum(partial_rows, 'tensor').astype(jnp.bfloat16)]
  transfers between devices with their start and end apart: 2 -> 0, of which waited for: 2 -> 0; matrix products, arithmetic and copies ran while one was open for 40% -> 0% of each run, Pallas kernels for 0% -> 0%
where the time goes in v1:
time: 55.9 us; the launch traced here: 55.6 us
  Pallas kernels  46.4 us (83%)
  local copies, waits for them, and re-layouts  7.62 us (14%)
  other arithmetic  0.9 us (2%)
  between operations  0.68 us (1%)
    pallas_call x1, Pallas kernels, entries_of(): pl.pallas_call(functools.partial(entries_kernel, adapters, tensors), out_...  25.6 us
    pallas_call x1, Pallas kernels, attend(): pl.pallas_call(attend_kernel, out_shape=jax.ShapeDtypeStruct(queries.shap...  20.8 us
    unnamed x14, local copies, waits for them, and re-layouts  7.62 us

profile of v1, /device:TPU:0, one launch (start us, length us, event | category | flops | bytes accessed | tf_op | source)
XLA Modules:
  0.0 55.6 jit_solution(16853318622068096044)
XLA Ops:
  0.6 0.7 %convert_element_type.9 = f32[32]{0:T(128)S(1)} convert(s32[32]{0:T(128)} %lengths.1) | non-fusion elementwise | flops 32 | bytes 256 | tf_op jit(solution)/shard_map/convert_element_type | solution.py:403
  1.3 0.1 fusion
  1.5 0.1 pad_maximum_fusion
  1.5 0.7 %copy.10.index_col = s32[32,1]{1,0:T(8,128)S(1)} copy(s32[32,1]{0,1:T(1,128)} %param.14) | data formatting | bytes 256 | tf_op args[6]
  2.3 0.0 copy-start
  2.3 1.2 %copy-done = bf16[1,4096,128]{2,1,0:T(8,128)(2,1)S(1)} copy-done((bf16[1,4096,128]{2,1,0:T(8,128)(2,1)S(1)}, bf16[1,4096,128]{2,1,0:T(8,128)(2,1)}, u32[]{:S(2)}) %copy-start) | copy-done | bytes 1048600
  3.5 0.0 copy-start.1
  3.5 0.9 %copy-done.1 = bf16[32,4096]{1,0:T(8,128)(2,1)S(1)} copy-done((bf16[32,4096]{1,0:T(8,128)(2,1)S(1)}, bf16[32,4096]{1,0:T(8,128)(2,1)}, u32[]{:S(2)}) %copy-start.1) | copy-done | bytes 262168
  4.4 0.0 copy-start.2
  4.5 0.9 %copy-done.2 = bf16[1,2,64,512]{3,2,1,0:T(8,128)(2,1)S(1)} copy-done((bf16[1,2,64,512]{3,2,1,0:T(8,128)(2,1)S(1)}, bf16[1,2,64,512]{3,2,1,0:T(8,128)(2,1)}, u32[]{:S(2)}) %copy-start.2) | copy-done | bytes 131096
  5.4 0.0 copy-start.3
  5.4 0.7 %copy-done.3 = s32[32,1]{0,1:T(1,128)S(1)} copy-done((s32[32,1]{0,1:T(1,128)S(1)}, s32[32,1]{0,1:T(1,128)}, u32[]{:S(2)}) %copy-start.3) | copy-done | bytes 152
  6.0 25.6 %entries.1 = f32[2,32,512]{2,1,0:T(8,128)S(1)} custom-call(bf16[32,4096]{1,0:T(8,128)(2,1)S(1)} %copy-done.1, bf16[8192,2,512]{2,1,0:T(2,128)(2,1)} %weight.1, bf16[1,4096,128]{2,1,0:T(8,128)(2,1)S(1)} %copy-done, bf16[1,2,64,512]{3,2,1,0:T(8,128)(2,1)S(1)} %copy-done.2, s32[32,1]{1,0:T(8,128)S(1)} %copy.10.index_col, s32[1,32]{1,0:T(1,128)S(1)} %bitcast.11, ...), custom_call_target="tpu_custom_call" | custom-call | tf_op jit(solution)/shard_map/entries/pallas_call | solution.py:270
  31.6 1.0 %copy.12 = bf16[4,8,32,128]{3,2,1,0:T(8,128)(2,1)S(1)} copy(bf16[4,8,32,128]{3,1,2,0:T(8,128)(2,1)} %bitcast.12) | data formatting | bytes 524288
  32.6 0.0 copy-start.4
  32.6 0.6 %copy-done.4 = s32[32]{0:T(128)S(1)} copy-done((s32[32]{0:T(128)S(1)}, s32[32]{0:T(128)}, u32[]{:S(2)}) %copy-start.4) | copy-done | bytes 152
  33.3 20.8 %attend.1 = bf16[32,32,128]{2,1,0:T(8,128)(2,1)S(1)} custom-call(s32[32]{0:T(128)S(1)} %copy-done.4, bf16[32,32,128]{2,1,0:T(8,128)(2,1)S(1)} %bitcast.10, bf16[32,2,512,512]{3,2,1,0:T(8,128)(2,1)} %cache.1, f32[2,32,512]{2,1,0:T(8,128)S(1)} %entries.1), custom_call_target="tpu_custom_call" | custom-call | tf_op jit(solution)/shard_map/attend/pallas_call | solution.py:379
  54.1 0.8 %copy.15 = bf16[4,8,32,128]{3,1,2,0:T(8,128)(2,1)} copy(bf16[4,8,32,128]{3,2,1,0:T(8,128)(2,1)S(1)} %bitcast.9) | data formatting | bytes 524288
  54.9 0.7 %copy.11 = bf16[32,2,512]{2,1,0:T(2,128)(2,1)} copy(bf16[32,2,512]{2,0,1:T(8,128)(2,1)S(1)} %convert_bitcast_fusion) | data formatting | bytes 131072
  (2 shorter events, 0.0 us)
Async XLA Ops:
  2.3 1.2 %copy-start = (bf16[1,4096,128]{2,1,0:T(8,128)(2,1)S(1)}, bf16[1,4096,128]{2,1,0:T(8,128)(2,1)}, u32[]{:S(2)}) copy-start(bf16[1,4096,128]{2,1,0:T(8,128)(2,1)} %down.1) | copy-start | bytes 3145732
  3.5 0.9 %copy-start.1 = (bf16[32,4096]{1,0:T(8,128)(2,1)S(1)}, bf16[32,4096]{1,0:T(8,128)(2,1)}, u32[]{:S(2)}) copy-start(bf16[32,4096]{1,0:T(8,128)(2,1)} %hidden.1) | copy-start | bytes 786436
  4.4 0.9 %copy-start.2 = (bf16[1,2,64,512]{3,2,1,0:T(8,128)(2,1)S(1)}, bf16[1,2,64,512]{3,2,1,0:T(8,128)(2,1)}, u32[]{:S(2)}) copy-start(bf16[1,2,64,512]{3,2,1,0:T(8,128)(2,1)} %up.1) | copy-start | bytes 393220
  5.4 0.7 %copy-start.3 = (s32[32,1]{0,1:T(1,128)S(1)}, s32[32,1]{0,1:T(1,128)}, u32[]{:S(2)}) copy-start(s32[32,1]{0,1:T(1,128)} %param.14) | copy-start | bytes 388
  32.6 0.7 %copy-start.4 = (s32[32]{0:T(128)S(1)}, s32[32]{0:T(128)}, u32[]{:S(2)}) copy-start(s32[32]{0:T(128)} %lengths.1) | copy-start | bytes 388

commit v2 on v1

--- a/solution.py
+++ b/solution.py
@@ -17,7 +17,8 @@
 DEPTH = 512
 SLOTS = 4
 CHUNK = 128
-AHEAD = 8
+AHEAD = 16
+TOGETHER = 4
 MESH = pl.DeviceIdType.MESH
 F32 = jnp.float32
 BF16 = jnp.bfloat16
@@ -300,7 +301,7 @@
 
 def attend_kernel(lengths, queries, cache, entries, out, held, sems):
     requests, lines, _ = queries.shape
-    context = cache.shape[2]
+    context, cols = cache.shape[2:]
     heads = lines // GROUP
     chunks = context // CHUNK
     scaling = HEAD_DIM ** -0.5
@@ -320,6 +321,10 @@
 
     for r in range(AHEAD):
         copies(r, lambda copy: copy.start())
+        for c in range(chunks):
+            @pl.when(c * CHUNK >= lengths[r])
+            def _():
+                held[r, 1, c * CHUNK : (c + 1) * CHUNK, :] = jnp.zeros((CHUNK, cols), BF16)
 
     owner = iota((lines, HEAD_DIM), 0) // GROUP
 
@@ -330,9 +335,8 @@
             chosen = jnp.where(owner == head, part, chosen)
         return chosen
 
-    def step(r, carry):
+    def one(r):
         slot = lax.rem(r, AHEAD)
-        copies(r, lambda copy: copy.wait())
         length = lengths[r]
         query = queries[r]
         apart = jnp.concatenate(
@@ -341,36 +345,35 @@
         own_score = jnp.sum(
             query.astype(F32) * own(entries[0, pl.ds(r, 1), :]), axis=1, keepdims=True
         ) * scaling
-        own_value = own(entries[1, pl.ds(r, 1), :])
-
-        for used in range(1, chunks + 1):
-            @pl.when((length > (used - 1) * CHUNK) & (length <= used * CHUNK))
+        scores = lax.dot_general(
+            apart, held[slot, 0], (((1,), (1,)), ((), ())), preferred_element_type=F32
+        ) * scaling
+        valid = iota((lines, context), 1) < length
+        scores = jnp.where(valid, scores, -1e30)
+        highest = jnp.maximum(jnp.max(scores, axis=1, keepdims=True), own_score)
+        weights = jnp.where(valid, jnp.exp(scores - highest), 0.0)
+        own_weight = jnp.exp(own_score - highest)
+        inverse = 1.0 / (jnp.sum(weights, axis=1, keepdims=True) + own_weight)
+        probs = (weights * inverse).astype(BF16)
+        own_prob = (own_weight * inverse).astype(BF16).astype(F32)
+        mixed = own(jnp.dot(probs, held[slot, 1], preferred_element_type=F32))
+        return (mixed + own_prob * own(entries[1, pl.ds(r, 1), :])).astype(BF16)
+
+    def step(n, carry):
+        base = n * TOGETHER
+        for k in range(TOGETHER):
+            copies(base + k, lambda copy: copy.wait())
+        results = [one(base + k) for k in range(TOGETHER)]
+        for k in range(TOGETHER):
+            out[base + k] = results[k]
+        for k in range(TOGETHER):
+            @pl.when(base + k + AHEAD < requests)
             def _():
-                size = used * CHUNK
-                scores = lax.dot_general(
-                    apart, held[slot, 0, :size, :], (((1,), (1,)), ((), ())),
-                    preferred_element_type=F32,
-                ) * scaling
-                valid = iota((lines, size), 1) < length
-                scores = jnp.where(valid, scores, -1e30)
-                highest = jnp.maximum(jnp.max(scores, axis=1, keepdims=True), own_score)
-                weights = jnp.where(valid, jnp.exp(scores - highest), 0.0)
-                own_weight = jnp.exp(own_score - highest)
-                inverse = 1.0 / (jnp.sum(weights, axis=1, keepdims=True) + own_weight)
-                probs = (weights * inverse).astype(BF16)
-                own_prob = (own_weight * inverse).astype(BF16).astype(F32)
-                mixed = own(
-                    jnp.dot(probs, held[slot, 1, :size, :], preferred_element_type=F32)
-                )
-                out[r] = (mixed + own_prob * own_value).astype(BF16)
-
-        @pl.when(r + AHEAD < requests)
-        def _():
-            copies(r + AHEAD, lambda copy: copy.start())
+                copies(base + k + AHEAD, lambda copy: copy.start())
 
         return carry
 
-    lax.fori_loop(0, requests, step, 0)
+    lax.fori_loop(0, requests // TOGETHER, step, 0)
 
 
 def attend(lengths, queries, cache, entries):

time: 55.9 us -> 54.6 us (0.977)
  Pallas kernels: 46.4 us -> 44.9 us
    pallas_call x1, Pallas kernels: 20.8 us -> 19.3 us  [attend(): pl.pallas_call(attend_kernel, out_shape=jax.ShapeDtypeStruct(queries.shap...]
where the time goes in v2:
time: 54.6 us; the launch traced here: 54.1 us
  Pallas kernels  44.9 us (82%)
  local copies, waits for them, and re-layouts  7.62 us (14%)
  other arithmetic  0.9 us (2%)
  between operations  0.68 us (1%)
    pallas_call x1, Pallas kernels, entries_of(): pl.pallas_call(functools.partial(entries_kernel, adapters, tensors), out_...  25.6 us
    pallas_call x1, Pallas kernels, attend(): pl.pallas_call(attend_kernel, out_shape=jax.ShapeDtypeStruct(queries.shap...  19.3 us
    unnamed x14, local copies, waits for them, and re-layouts  7.62 us

profile of v2, /device:TPU:0, one launch (start us, length us, event | category | flops | bytes accessed | tf_op | source)
XLA Modules:
  0.0 54.1 jit_solution(6668073456995877023)
XLA Ops:
  0.6 0.7 %convert_element_type.9 = f32[32]{0:T(128)S(1)} convert(s32[32]{0:T(128)} %lengths.1) | non-fusion elementwise | flops 32 | bytes 256 | tf_op jit(solution)/shard_map/convert_element_type | solution.py:406
  1.3 0.1 fusion
  1.5 0.1 pad_maximum_fusion
  1.5 0.7 %copy.10.index_col = s32[32,1]{1,0:T(8,128)S(1)} copy(s32[32,1]{0,1:T(1,128)} %param.14) | data formatting | bytes 256 | tf_op args[6]
  2.3 0.0 copy-start
  2.3 1.2 %copy-done = bf16[1,4096,128]{2,1,0:T(8,128)(2,1)S(1)} copy-done((bf16[1,4096,128]{2,1,0:T(8,128)(2,1)S(1)}, bf16[1,4096,128]{2,1,0:T(8,128)(2,1)}, u32[]{:S(2)}) %copy-start) | copy-done | bytes 1048600
  3.5 0.0 copy-start.1
  3.5 0.9 %copy-done.1 = bf16[32,4096]{1,0:T(8,128)(2,1)S(1)} copy-done((bf16[32,4096]{1,0:T(8,128)(2,1)S(1)}, bf16[32,4096]{1,0:T(8,128)(2,1)}, u32[]{:S(2)}) %copy-start.1) | copy-done | bytes 262168
  4.4 0.0 copy-start.2
  4.5 0.9 %copy-done.2 = bf16[1,2,64,512]{3,2,1,0:T(8,128)(2,1)S(1)} copy-done((bf16[1,2,64,512]{3,2,1,0:T(8,128)(2,1)S(1)}, bf16[1,2,64,512]{3,2,1,0:T(8,128)(2,1)}, u32[]{:S(2)}) %copy-start.2) | copy-done | bytes 131096
  5.4 0.0 copy-start.3
  5.4 0.7 %copy-done.3 = s32[32,1]{0,1:T(1,128)S(1)} copy-done((s32[32,1]{0,1:T(1,128)S(1)}, s32[32,1]{0,1:T(1,128)}, u32[]{:S(2)}) %copy-start.3) | copy-done | bytes 152
  6.0 25.6 %entries.1 = f32[2,32,512]{2,1,0:T(8,128)S(1)} custom-call(bf16[32,4096]{1,0:T(8,128)(2,1)S(1)} %copy-done.1, bf16[8192,2,512]{2,1,0:T(2,128)(2,1)} %weight.1, bf16[1,4096,128]{2,1,0:T(8,128)(2,1)S(1)} %copy-done, bf16[1,2,64,512]{3,2,1,0:T(8,128)(2,1)S(1)} %copy-done.2, s32[32,1]{1,0:T(8,128)S(1)} %copy.10.index_col, s32[1,32]{1,0:T(1,128)S(1)} %bitcast.11, ...), custom_call_target="tpu_custom_call" | custom-call | tf_op jit(solution)/shard_map/entries/pallas_call | solution.py:271
  31.6 1.0 %copy.12 = bf16[4,8,32,128]{3,2,1,0:T(8,128)(2,1)S(1)} copy(bf16[4,8,32,128]{3,1,2,0:T(8,128)(2,1)} %bitcast.12) | data formatting | bytes 524288
  32.6 0.0 copy-start.4
  32.6 0.6 %copy-done.4 = s32[32]{0:T(128)S(1)} copy-done((s32[32]{0:T(128)S(1)}, s32[32]{0:T(128)}, u32[]{:S(2)}) %copy-start.4) | copy-done | bytes 152
  33.3 19.3 %attend.1 = bf16[32,32,128]{2,1,0:T(8,128)(2,1)S(1)} custom-call(s32[32]{0:T(128)S(1)} %copy-done.4, bf16[32,32,128]{2,1,0:T(8,128)(2,1)S(1)} %bitcast.10, bf16[32,2,512,512]{3,2,1,0:T(8,128)(2,1)} %cache.1, f32[2,32,512]{2,1,0:T(8,128)S(1)} %entries.1), custom_call_target="tpu_custom_call" | custom-call | tf_op jit(solution)/shard_map/attend/pallas_call | solution.py:382
  52.6 0.8 %copy.15 = bf16[4,8,32,128]{3,1,2,0:T(8,128)(2,1)} copy(bf16[4,8,32,128]{3,2,1,0:T(8,128)(2,1)S(1)} %bitcast.9) | data formatting | bytes 524288
  53.4 0.7 %copy.11 = bf16[32,2,512]{2,1,0:T(2,128)(2,1)} copy(bf16[32,2,512]{2,0,1:T(8,128)(2,1)S(1)} %convert_bitcast_fusion) | data formatting | bytes 131072
  (2 shorter events, 0.0 us)
Async XLA Ops:
  2.3 1.2 %copy-start = (bf16[1,4096,128]{2,1,0:T(8,128)(2,1)S(1)}, bf16[1,4096,128]{2,1,0:T(8,128)(2,1)}, u32[]{:S(2)}) copy-start(bf16[1,4096,128]{2,1,0:T(8,128)(2,1)} %down.1) | copy-start | bytes 3145732
  3.5 0.9 %copy-start.1 = (bf16[32,4096]{1,0:T(8,128)(2,1)S(1)}, bf16[32,4096]{1,0:T(8,128)(2,1)}, u32[]{:S(2)}) copy-start(bf16[32,4096]{1,0:T(8,128)(2,1)} %hidden.1) | copy-start | bytes 786436
  4.4 0.9 %copy-start.2 = (bf16[1,2,64,512]{3,2,1,0:T(8,128)(2,1)S(1)}, bf16[1,2,64,512]{3,2,1,0:T(8,128)(2,1)}, u32[]{:S(2)}) copy-start(bf16[1,2,64,512]{3,2,1,0:T(8,128)(2,1)} %up.1) | copy-start | bytes 393220
  5.4 0.7 %copy-start.3 = (s32[32,1]{0,1:T(1,128)S(1)}, s32[32,1]{0,1:T(1,128)}, u32[]{:S(2)}) copy-start(s32[32,1]{0,1:T(1,128)} %param.14) | copy-start | bytes 388
  32.6 0.7 %copy-start.4 = (s32[32]{0:T(128)S(1)}, s32[32]{0:T(128)}, u32[]{:S(2)}) copy-start(s32[32]{0:T(128)} %lengths.1) | copy-start | bytes 388

commit v3 on v2

--- a/solution.py
+++ b/solution.py
@@ -146,8 +146,9 @@
             slot = lax.rem(n, SLOTS)
             start = pl.multiple_of(lax.rem(n, per_source) * 2 * DEPTH, 2 * DEPTH)
             features = wide[:, pl.ds(start, 2 * DEPTH)]
-            for tile, copy in enumerate(block_copies(n)):
+            for copy in block_copies(n):
                 copy.wait()
+            for tile in range(tiles):
                 total[:, tile * 128 : (tile + 1) * 128] += jnp.dot(
                     features,
                     blocks.at[slot, tile].reshape(2 * DEPTH, 128)[...],

time: 54.6 us -> 50.5 us (0.925)
  Pallas kernels: 44.9 us -> 41 us
    pallas_call x1, Pallas kernels: 25.6 us -> 21.4 us  [entries_of(): pl.pallas_call(functools.partial(entries_kernel, adapters, tensors), out_...]
where the time goes in v3:
time: 50.5 us; the launch traced here: 50.2 us
  Pallas kernels  41 us (81%)
  local copies, waits for them, and re-layouts  7.62 us (15%)
  other arithmetic  0.9 us (2%)
  between operations  0.68 us (1%)
    pallas_call x1, Pallas kernels, entries_of(): pl.pallas_call(functools.partial(entries_kernel, adapters, tensors), out_...  21.4 us
    pallas_call x1, Pallas kernels, attend(): pl.pallas_call(attend_kernel, out_shape=jax.ShapeDtypeStruct(queries.shap...  19.6 us
    unnamed x14, local copies, waits for them, and re-layouts  7.62 us

profile of v3, /device:TPU:0, one launch (start us, length us, event | category | flops | bytes accessed | tf_op | source)
XLA Modules:
  0.0 50.2 jit_solution(16620425154202495293)
XLA Ops:
  0.6 0.7 %convert_element_type.9 = f32[32]{0:T(128)S(1)} convert(s32[32]{0:T(128)} %lengths.1) | non-fusion elementwise | flops 32 | bytes 256 | tf_op jit(solution)/shard_map/convert_element_type | solution.py:407
  1.3 0.1 fusion
  1.5 0.1 pad_maximum_fusion
  1.5 0.7 %copy.10.index_col = s32[32,1]{1,0:T(8,128)S(1)} copy(s32[32,1]{0,1:T(1,128)} %param.14) | data formatting | bytes 256 | tf_op args[6]
  2.3 0.0 copy-start
  2.3 1.2 %copy-done = bf16[1,4096,128]{2,1,0:T(8,128)(2,1)S(1)} copy-done((bf16[1,4096,128]{2,1,0:T(8,128)(2,1)S(1)}, bf16[1,4096,128]{2,1,0:T(8,128)(2,1)}, u32[]{:S(2)}) %copy-start) | copy-done | bytes 1048600
  3.5 0.0 copy-start.1
  3.5 0.9 %copy-done.1 = bf16[32,4096]{1,0:T(8,128)(2,1)S(1)} copy-done((bf16[32,4096]{1,0:T(8,128)(2,1)S(1)}, bf16[32,4096]{1,0:T(8,128)(2,1)}, u32[]{:S(2)}) %copy-start.1) | copy-done | bytes 262168
  4.4 0.0 copy-start.2
  4.5 0.9 %copy-done.2 = bf16[1,2,64,512]{3,2,1,0:T(8,128)(2,1)S(1)} copy-done((bf16[1,2,64,512]{3,2,1,0:T(8,128)(2,1)S(1)}, bf16[1,2,64,512]{3,2,1,0:T(8,128)(2,1)}, u32[]{:S(2)}) %copy-start.2) | copy-done | bytes 131096
  5.4 0.0 copy-start.3
  5.4 0.7 %copy-done.3 = s32[32,1]{0,1:T(1,128)S(1)} copy-done((s32[32,1]{0,1:T(1,128)S(1)}, s32[32,1]{0,1:T(1,128)}, u32[]{:S(2)}) %copy-start.3) | copy-done | bytes 152
  6.0 21.4 %entries.1 = f32[2,32,512]{2,1,0:T(8,128)S(1)} custom-call(bf16[32,4096]{1,0:T(8,128)(2,1)S(1)} %copy-done.1, bf16[8192,2,512]{2,1,0:T(2,128)(2,1)} %weight.1, bf16[1,4096,128]{2,1,0:T(8,128)(2,1)S(1)} %copy-done, bf16[1,2,64,512]{3,2,1,0:T(8,128)(2,1)S(1)} %copy-done.2, s32[32,1]{1,0:T(8,128)S(1)} %copy.10.index_col, s32[1,32]{1,0:T(1,128)S(1)} %bitcast.11, ...), custom_call_target="tpu_custom_call" | custom-call | tf_op jit(solution)/shard_map/entries/pallas_call | solution.py:272
  27.5 1.0 %copy.12 = bf16[4,8,32,128]{3,2,1,0:T(8,128)(2,1)S(1)} copy(bf16[4,8,32,128]{3,1,2,0:T(8,128)(2,1)} %bitcast.12) | data formatting | bytes 524288
  28.5 0.0 copy-start.4
  28.5 0.6 %copy-done.4 = s32[32]{0:T(128)S(1)} copy-done((s32[32]{0:T(128)S(1)}, s32[32]{0:T(128)}, u32[]{:S(2)}) %copy-start.4) | copy-done | bytes 152
  29.1 19.6 %attend.1 = bf16[32,32,128]{2,1,0:T(8,128)(2,1)S(1)} custom-call(s32[32]{0:T(128)S(1)} %copy-done.4, bf16[32,32,128]{2,1,0:T(8,128)(2,1)S(1)} %bitcast.10, bf16[32,2,512,512]{3,2,1,0:T(8,128)(2,1)} %cache.1, f32[2,32,512]{2,1,0:T(8,128)S(1)} %entries.1), custom_call_target="tpu_custom_call" | custom-call | tf_op jit(solution)/shard_map/attend/pallas_call | solution.py:383
  48.7 0.8 %copy.15 = bf16[4,8,32,128]{3,1,2,0:T(8,128)(2,1)} copy(bf16[4,8,32,128]{3,2,1,0:T(8,128)(2,1)S(1)} %bitcast.9) | data formatting | bytes 524288
  49.5 0.7 %copy.11 = bf16[32,2,512]{2,1,0:T(2,128)(2,1)} copy(bf16[32,2,512]{2,0,1:T(8,128)(2,1)S(1)} %convert_bitcast_fusion) | data formatting | bytes 131072
  (2 shorter events, 0.0 us)
Async XLA Ops:
  2.3 1.2 %copy-start = (bf16[1,4096,128]{2,1,0:T(8,128)(2,1)S(1)}, bf16[1,4096,128]{2,1,0:T(8,128)(2,1)}, u32[]{:S(2)}) copy-start(bf16[1,4096,128]{2,1,0:T(8,128)(2,1)} %down.1) | copy-start | bytes 3145732
  3.5 0.9 %copy-start.1 = (bf16[32,4096]{1,0:T(8,128)(2,1)S(1)}, bf16[32,4096]{1,0:T(8,128)(2,1)}, u32[]{:S(2)}) copy-start(bf16[32,4096]{1,0:T(8,128)(2,1)} %hidden.1) | copy-start | bytes 786436
  4.4 0.9 %copy-start.2 = (bf16[1,2,64,512]{3,2,1,0:T(8,128)(2,1)S(1)}, bf16[1,2,64,512]{3,2,1,0:T(8,128)(2,1)}, u32[]{:S(2)}) copy-start(bf16[1,2,64,512]{3,2,1,0:T(8,128)(2,1)} %up.1) | copy-start | bytes 393220
  5.4 0.7 %copy-start.3 = (s32[32,1]{0,1:T(1,128)S(1)}, s32[32,1]{0,1:T(1,128)}, u32[]{:S(2)}) copy-start(s32[32,1]{0,1:T(1,128)} %param.14) | copy-start | bytes 388
  28.5 0.7 %copy-start.4 = (s32[32]{0:T(128)S(1)}, s32[32]{0:T(128)}, u32[]{:S(2)}) copy-start(s32[32]{0:T(128)} %lengths.1) | copy-start | bytes 388
